TPU v7x, 32 devices: a whole 2x2x4 slice. The times are simulated.
32 devices in a mesh: node: 4 (over y, x), local: 2 (over core), edata: 4 (over z).
Axes of the slice: x: 2, y: 2, z: 4, core: 2. Of those that a mesh axis runs over, the one named last changes fastest.
Arguments:
- tokens: bfloat16 [2048, 4096], P(('node', 'local'), 'edata'), may hold values from -6 to 6
- grad_out: bfloat16 [2048, 4096], P(('node', 'local'), 'edata'), may hold values from -0.59765625 to 0.59765625
- routes: int32 [2048, 2], P(('node', 'local')), may hold values from 0 to 63, all different within a row
- gates: bfloat16 [2048, 2], P(('node', 'local')), may hold values from 0.099609375 to 1
- w_in: bfloat16 [4096, 2048], P('edata', ('node', 'local')), may hold values from -0.09375 to 0.09375
- w_out: bfloat16 [2048, 4096], P(('node', 'local'), 'edata'), may hold values from -0.09375 to 0.09375
Outputs:
- grad_tokens: bfloat16 [2048, 4096], P(('node', 'local'), 'edata')
- grad_gates: float32 [2048, 2], P(('node', 'local'))
- grad_w_in: float32 [4096, 2048], P('edata', ('node', 'local'))
- grad_w_out: float32 [2048, 4096], P(('node', 'local'), 'edata')
Inputs may be any that keep to these rules, and one draw needn't show every extreme that they name: `routes`: each token names two different experts.
All inputs are finite; a program needn't handle non-finite values.
Results may differ from a plain program's by a relative error of at most 0.0049.
Values may be sent and summed in bfloat16 or wider, within the bound.
No kernel may reach another device: no remote copies, remote signals or barrier semaphores. Data moves between devices by JAX's collectives and lax.ppermute only.
A program may use at most 64 MiB of HBM per device.

v0:
```python
import jax
import jax.numpy as jnp
from jax import lax
from jax.sharding import PartitionSpec as P

EXPERTS = 64
WINDOW = 2


def gelu_pair(pre_act):
    coefficient = 0.7978845608028654
    inner_arg = coefficient * (pre_act + 0.044715 * pre_act * pre_act * pre_act)
    tanh_val = jnp.tanh(inner_arg)
    activation = 0.5 * pre_act * (1.0 + tanh_val)
    slopes = 0.5 * (1.0 + tanh_val) + 0.5 * pre_act * (1.0 - tanh_val * tanh_val) * coefficient * (
        1.0 + 3.0 * 0.044715 * pre_act * pre_act
    )
    return (activation, slopes)


def body(tokens, grad_out, routes, gates, w_in, w_out):
    n_node = lax.axis_size("node")
    n_local = lax.axis_size("local")
    groups = n_node * n_local
    half_nodes = n_node // WINDOW
    tok_rows = tokens.shape[0]
    shard_cols = tokens.shape[1]
    capacity = 2 * tok_rows // EXPERTS
    slots = WINDOW * capacity
    flat_routes = routes.reshape(-1)
    in_window = (flat_routes[:, None] == jnp.arange(WINDOW, dtype=jnp.int32)[None, :]).astype(
        jnp.int32
    )
    before = jnp.cumsum(in_window, axis=0) - in_window
    position = jnp.sum(before * in_window, axis=1)
    live_pair = (flat_routes < WINDOW) & (position < capacity)
    slot_index = jnp.where(live_pair, flat_routes * capacity + position, -1)
    matches = slot_index[:, None] == jnp.arange(slots, dtype=jnp.int32)[None, :]
    placing = jnp.any(matches.reshape(tok_rows, 2, slots), axis=1).astype(jnp.bfloat16).T
    send_x = jnp.dot(placing, tokens, preferred_element_type=jnp.float32).astype(jnp.bfloat16)
    send_dy = jnp.dot(placing, grad_out, preferred_element_type=jnp.float32).astype(jnp.bfloat16)
    gate_flat = gates.reshape(-1)
    send_gate = jnp.sum(jnp.where(matches, gate_flat[:, None], jnp.zeros((), gates.dtype)), axis=0)
    spread_x = jnp.repeat(send_x.reshape(WINDOW, capacity, shard_cols), half_nodes, axis=0)
    spread_dy = jnp.repeat(send_dy.reshape(WINDOW, capacity, shard_cols), half_nodes, axis=0)
    spread_gate = jnp.repeat(send_gate.reshape(WINDOW, capacity), half_nodes, axis=0)
    got_x, got_dy, got_gate = (
        lax.all_to_all(spread_x, "node", split_axis=0, concat_axis=0, tiled=True),
        lax.all_to_all(spread_dy, "node", split_axis=0, concat_axis=0, tiled=True),
        lax.all_to_all(spread_gate, "node", split_axis=0, concat_axis=0, tiled=True),
    )
    rows_x, rows_dy, rows_gate = (
        lax.all_gather(got_x[:, None], "local", axis=1, tiled=True),
        lax.all_gather(got_dy[:, None], "local", axis=1, tiled=True),
        lax.all_gather(got_gate[:, None], "local", axis=1, tiled=True),
    )
    total_rows = groups * capacity
    x_rows = rows_x.reshape(total_rows, shard_cols)
    dy_rows = rows_dy.reshape(total_rows, shard_cols)
    gate_col = rows_gate.reshape(total_rows).astype(jnp.float32)[:, None]
    pre_part = jnp.dot(x_rows, w_in, preferred_element_type=jnp.float32)
    back_part = lax.dot_general(
        dy_rows, w_out, (((1,), (1,)), ((), ())), preferred_element_type=jnp.float32
    )
    pre_act, back_grad = lax.psum((pre_part, back_part), "edata")
    activation, slopes = gelu_pair(pre_act)
    scaled = (gate_col * activation).astype(jnp.bfloat16)
    grad_w_out = lax.dot_general(
        scaled, dy_rows, (((0,), (0,)), ((), ())), preferred_element_type=jnp.float32
    )
    pre_grad = (gate_col * back_grad * slopes).astype(jnp.bfloat16)
    grad_w_in = lax.dot_general(
        x_rows, pre_grad, (((0,), (0,)), ((), ())), preferred_element_type=jnp.float32
    )
    token_part = lax.dot_general(
        pre_grad, w_in, (((1,), (1,)), ((), ())), preferred_element_type=jnp.float32
    )
    gate_part = jnp.sum(activation * back_grad, axis=1)
    token_part = token_part.reshape(n_node, n_local, capacity, shard_cols)
    gate_part = gate_part.reshape(n_node, n_local, capacity)
    reduced_x, reduced_gate = (
        lax.psum_scatter(token_part, "local", scatter_dimension=1, tiled=True),
        lax.psum_scatter(gate_part, "local", scatter_dimension=1, tiled=True),
    )
    came_x, came_gate = (
        lax.all_to_all(reduced_x, "node", split_axis=0, concat_axis=0, tiled=True),
        lax.all_to_all(reduced_gate, "node", split_axis=0, concat_axis=0, tiled=True),
    )
    slot_grad = jnp.sum(came_x.reshape(WINDOW, half_nodes, capacity, shard_cols), axis=1)
    slot_gate = jnp.sum(came_gate.reshape(WINDOW, half_nodes, capacity), axis=1)
    slot_grad = slot_grad.reshape(slots, shard_cols)
    slot_gate = slot_gate.reshape(slots)
    safe_index = jnp.maximum(slot_index, 0)
    picked = slot_grad[safe_index].reshape(tok_rows, 2, shard_cols)
    keep_pair = live_pair.reshape(tok_rows, 2)
    grad_tokens = jnp.sum(
        jnp.where(keep_pair[:, :, None], picked, jnp.zeros((), jnp.float32)), axis=1
    ).astype(jnp.bfloat16)
    grad_gates = jnp.where(
        keep_pair, slot_gate[safe_index].reshape(tok_rows, 2), jnp.zeros((), jnp.float32)
    )
    return (grad_tokens, grad_gates, grad_w_in, grad_w_out)


def solution(mesh):
    in_specs = (
        P(("node", "local"), "edata"),
        P(("node", "local"), "edata"),
        P(("node", "local"), None),
        P(("node", "local"), None),
        P("edata", ("node", "local")),
        P(("node", "local"), "edata"),
    )
    out_specs = (
        P(("node", "local"), "edata"),
        P(("node", "local"), None),
        P("edata", ("node", "local")),
        P(("node", "local"), "edata"),
    )
    return jax.shard_map(body, mesh=mesh, in_specs=in_specs, out_specs=out_specs, check_vma=False)
```

profile of v0, /device:TPU:0, one launch (start us, length us, event | category | flops | bytes accessed | tf_op | source)
XLA Modules:
  0.0 135.5 jit_solution(7730568335097662634)
XLA Ops:
  7.2 0.0 copy-start
  7.2 0.9 copy.41
  8.1 0.1 eq.49
  8.3 0.1 eq.45
  8.4 0.6 reduce-window.6
  9.1 0.2 slice_reduce_fusion
  9.3 0.2 reduce-window.9
  9.5 0.1 add_bitcast_fusion
  9.6 0.1 reduce_sum.62
  9.7 0.1 add_select_fusion
  9.8 0.0 copy-start.5
  9.8 0.1 copy.49
  9.9 1.2 fusion
  11.1 0.6 broadcast_in_dim.67
  11.8 5.2 %all-to-all-start.1 = ((bf16[4,8,1024]{2,1,0:T(8,128)(2,1)}), bf16[4,8,1024]{2,1,0:T(8,128)(2,1)S(1)}, u32[]{:S(2)}, u32[]{:S(2)}) async-start(bf16[4,8,1024]{2,1,0:T(8,128)(2,1)} %bitcast.3), calls=%async_computation.1 | async-start | bytes 131072 | tf_op jit(solution)/shard_map/all_to_all | solution.py:49
  16.9 0.2 fusion.1
  17.1 0.1 copy.44
  17.3 0.2 broadcast_in_dim.62
  17.4 0.1 fusion.13
  17.5 0.1 reshape.154
  17.6 0.6 copy.45
  18.2 0.1 lt.56
  18.4 0.1 mul.108
  18.5 3.2 %all-to-all-done.1 = bf16[4,8,1024]{2,1,0:T(8,128)(2,1)S(1)} async-done(((bf16[4,8,1024]{2,1,0:T(8,128)(2,1)}), bf16[4,8,1024]{2,1,0:T(8,128)(2,1)S(1)}, u32[]{:S(2)}, u32[]{:S(2)}) %all-to-all-start.1) | async-done | bytes 65568 | tf_op jit(solution)/shard_map/all_to_all | solution.py:49
  21.8 0.6 broadcast_in_dim.69
  22.4 3.3 %all-to-all-start.2 = ((bf16[4,8,1024]{2,1,0:T(8,128)(2,1)}), bf16[4,8,1024]{2,1,0:T(8,128)(2,1)S(1)}, u32[]{:S(2)}, u32[]{:S(2)}) async-start(bf16[4,8,1024]{2,1,0:T(8,128)(2,1)} %bitcast.6), calls=%async_computation.2 | async-start | bytes 131072 | tf_op jit(solution)/shard_map/all_to_all | solution.py:48
  25.7 1.9 %all-gather = bf16[4,16,1024]{2,1,0:T(8,128)(2,1)S(1)} all-gather(bf16[4,8,1024]{2,1,0:T(8,128)(2,1)S(1)} %all-to-all-done.1), channel_id=2, replica_groups=mesh['node'=4,'local'=2,'edata'=4] {'local'}, dimensions={1}, use_global_device_ids=true | all-gather | bytes 196608 | tf_op jit(solution)/shard_map/all_gather | solution.py:54
  27.6 0.0 copy-done.2
  27.6 0.9 fusion.24
  28.5 2.0 %all-to-all-done.2 = bf16[4,8,1024]{2,1,0:T(8,128)(2,1)S(1)} async-done(((bf16[4,8,1024]{2,1,0:T(8,128)(2,1)}), bf16[4,8,1024]{2,1,0:T(8,128)(2,1)S(1)}, u32[]{:S(2)}, u32[]{:S(2)}) %all-to-all-start.2) | async-done | bytes 65568 | tf_op jit(solution)/shard_map/all_to_all | solution.py:48
  30.5 3.2 %all-to-all-start = ((bf16[4,1,8]{2,1,0:T(2,128)(2,1)}), bf16[4,1,8]{2,1,0:T(2,128)(2,1)S(1)}, u32[]{:S(2)}, u32[]{:S(2)}) async-start(bf16[4,1,8]{2,1,0:T(2,128)(2,1)} %copy.45), calls=%async_computation | async-start | bytes 4096 | tf_op jit(solution)/shard_map/all_to_all | solution.py:50
  33.7 0.0 all-reduce.8.cloned.1.call-start
  33.8 1.9 %all-gather.1 = bf16[4,16,1024]{2,1,0:T(8,128)(2,1)S(1)} all-gather(bf16[4,8,1024]{2,1,0:T(8,128)(2,1)S(1)} %all-to-all-done.2), channel_id=3, replica_groups=mesh['node'=4,'local'=2,'edata'=4] {'local'}, dimensions={1}, use_global_device_ids=true | all-gather | bytes 196608 | tf_op jit(solution)/shard_map/all_gather | solution.py:53
  35.7 0.8 fusion.25
  36.5 0.0 all-reduce.8.cloned.1.call-update
  36.6 1.7 %all-to-all-done = bf16[4,1,8]{2,1,0:T(2,128)(2,1)S(1)} async-done(((bf16[4,1,8]{2,1,0:T(2,128)(2,1)}), bf16[4,1,8]{2,1,0:T(2,128)(2,1)S(1)}, u32[]{:S(2)}, u32[]{:S(2)}) %all-to-all-start) | async-done | bytes 96 | tf_op jit(solution)/shard_map/all_to_all | solution.py:50
  38.3 0.0 copy-done.5
  38.3 0.6 dynamic-slice
  38.9 1.8 %all_gather.9 = bf16[4,2,8]{2,0,1:T(4,128)(2,1)S(1)} all-gather(bf16[4,1,8]{2,0,1:T(4,128)(2,1)S(1)} %copy.46), channel_id=1, replica_groups=mesh['node'=4,'local'=2,'edata'=4] {'local'}, dimensions={1}, use_global_device_ids=true | all-gather | bytes 192 | tf_op jit(solution)/shard_map/all_gather | solution.py:55
  40.7 0.1 reshape.169
  40.8 33.0 %all-reduce.8.cloned.1.call-done = (f32[64,256]{1,0:T(8,128)}, f32[64,256]{1,0:T(8,128)}) async-done(((f32[64,256]{1,0:T(8,128)}, f32[64,256]{1,0:T(8,128)}), (f32[64,256]{1,0:T(8,128)}, f32[64,256]{1,0:T(8,128)})) %all-reduce.8.cloned.1.call-update) | async-done | bytes 131088 | tf_op jit(solution)/shard_map/psum | solution.py:65
  73.8 1.1 multiply_reduce_fusion
  74.9 1.0 fusion.26
  75.9 1.3 fusion.27
  77.2 0.0 copy-done.3
  77.2 1.4 fusion.9
  78.5 0.1 reshape.165
  78.6 2.5 %all-reduce.1 = f32[4,2,8]{2,0,1:T(4,128)S(1)} all-reduce(f32[4,2,8]{2,0,1:T(4,128)S(1)} %copy.50), channel_id=5, replica_groups=mesh['node'=4,'local'=2,'edata'=4] {'local'}, use_global_device_ids=true, to_apply=%region_11.12.clone | all-reduce | flops 64 | bytes 512
  81.1 1.2 constant_dynamic-slice_fusion
  82.3 3.6 %all-to-all-start.4 = ((f32[4,1,8]{2,1,0:T(1,128)}), f32[4,1,8]{2,1,0:T(1,128)S(1)}, u32[]{:S(2)}, u32[]{:S(2)}) async-start(f32[4,1,8]{2,1,0:T(1,128)} %bitcast.13), calls=%async_computation.4 | async-start | bytes 4096 | tf_op jit(solution)/shard_map/all_to_all | solution.py:87
  85.9 0.7 all-reduce.6.cloned.1.call-update
  86.6 3.8 %all-to-all-done.4 = f32[4,1,8]{2,1,0:T(1,128)S(1)} async-done(((f32[4,1,8]{2,1,0:T(1,128)}), f32[4,1,8]{2,1,0:T(1,128)S(1)}, u32[]{:S(2)}, u32[]{:S(2)}) %all-to-all-start.4) | async-done | bytes 160 | tf_op jit(solution)/shard_map/all_to_all | solution.py:87
  90.5 0.1 reshape.167
  90.5 0.7 fusion.23
  91.3 10.1 %select_select_fusion = f32[512]{0:T(512)S(1)} fusion(s32[512]{0:T(512)S(1)} %bitcast.78, f32[]{:T(128)} %bitcast.15, f32[]{:T(128)} %bitcast.16, f32[]{:T(128)} %bitcast.17, f32[]{:T(128)} %bitcast.18, f32[]{:T(128)} %bitcast.19, f32[]{:T(128)} %bitcast.20, f32[]{:T(128)} %bitcast.21, f32[]{:T(128)} %bitcast.22, f32[]{:T(128)} %bitcast.23, f32[]{:T(128)} %bitcast.24, ...), kind=kLoop, calls=%fused_computation.41 | loop fusion | flops 15360 | bytes 4160 | tf_op jit(solution)/shard_map/gather | solution.py:100
  101.4 0.1 reshape.168
  101.5 6.8 %all-reduce.6.cloned.1.call-done = f32[4,2,8,1024]{3,2,1,0:T(8,128)} async-done(((f32[4,2,8,1024]{3,2,1,0:T(8,128)}), f32[4,2,8,1024]{3,2,1,0:T(8,128)}) %all-reduce.6.cloned.1.call-update) | async-done | bytes 262160
  108.3 2.2 %constant_dynamic-slice_fusion.1 = f32[4,1,8,1024]{3,2,1,0:T(8,128)} fusion(f32[4,2,8,1024]{3,2,1,0:T(8,128)} %all-reduce.6.cloned.1.call-done, u32[]{:T(128)} %bitcast.33), kind=kLoop, calls=%fused_computation.45 | loop fusion | bytes 262148
  110.5 3.9 %all-to-all-start.3 = ((f32[4,1,8,1024]{3,2,1,0:T(8,128)}), f32[4,1,8,1024]{3,2,1,0:T(8,128)S(1)}, u32[]{:S(2)}, u32[]{:S(2)}) async-start(f32[4,1,8,1024]{3,2,1,0:T(8,128)} %constant_dynamic-slice_fusion.1), calls=%async_computation.3 | async-start | bytes 262144 | tf_op jit(solution)/shard_map/all_to_all | solution.py:86
  114.4 0.7 copy.52
  115.1 4.3 %all-to-all-done.3 = f32[4,1,8,1024]{3,2,1,0:T(8,128)S(1)} async-done(((f32[4,1,8,1024]{3,2,1,0:T(8,128)}), f32[4,1,8,1024]{3,2,1,0:T(8,128)S(1)}, u32[]{:S(2)}, u32[]{:S(2)}) %all-to-all-start.3) | async-done | bytes 131104 | tf_op jit(solution)/shard_map/all_to_all | solution.py:86
  119.4 1.9 %gather_fusion = f32[512,1024]{1,0:T(8,128)S(1)} fusion(f32[16,1024]{1,0:T(8,128)S(1)} %bitcast.69, s32[1024]{0:T(1024)S(1)} %pad_clamp_fusion), kind=kCustom, calls=%fused_computation | custom fusion | bytes 4196352 | tf_op jit(solution)/shard_map/gather | solution.py:94
  121.3 2.3 %reshape.164 = f32[256,2,1024]{2,1,0:T(2,128)} reshape(f32[512,1024]{1,0:T(8,128)S(1)} %gather_fusion) | data formatting | bytes 4194304 | tf_op jit(solution)/shard_map/reshape | solution.py:94
  123.6 5.0 %select_reduce_fusion = bf16[256,1024]{1,0:T(8,128)(2,1)} fusion(f32[256,2,1024]{2,1,0:T(2,128)} %reshape.164, pred[256,2]{1,0:T(8,128)(4,1)S(1)} %get-tuple-element.23), kind=kLoop, calls=%fused_computation.1 | loop fusion | flops 786432 | bytes 2621952 | tf_op jit(solution)/shard_map/reduce_sum | solution.py:96
  (21 shorter events, 0.1 us)
Async XLA Ops:
  7.2 28.5 %copy-start = (bf16[1024,256]{1,0:T(8,128)(2,1)S(1)}, bf16[1024,256]{1,0:T(8,128)(2,1)}, u32[]{:S(2)}) copy-start(bf16[1024,256]{1,0:T(8,128)(2,1)} %param.10) | copy-start | bytes 1572868
  7.2 9.8 %copy-start.1 = (bf16[256,1024]{1,0:T(8,128)(2,1)S(1)}, bf16[256,1024]{1,0:T(8,128)(2,1)}, u32[]{:S(2)}) copy-start(bf16[256,1024]{1,0:T(8,128)(2,1)} %param.6) | copy-start | bytes 1572868
  7.2 9.9 %copy-start.4 = (bf16[256,2]{0,1:T(2,128)(2,1)S(1)}, bf16[256,2]{0,1:T(2,128)(2,1)}, u32[]{:S(2)}) copy-start(bf16[256,2]{0,1:T(2,128)(2,1)} %param.9) | copy-start | bytes 3076
  7.2 20.4 %copy-start.2 = (bf16[256,1024]{1,0:T(8,128)(2,1)S(1)}, bf16[256,1024]{1,0:T(8,128)(2,1)}, u32[]{:S(2)}) copy-start(bf16[256,1024]{1,0:T(8,128)(2,1)} %param.11) | copy-start | bytes 1572868
  9.8 28.5 %copy-start.5 = (u32[32]{0:T(128)S(1)}, u32[32]{0:T(128)}, u32[]{:S(2)}) copy-start(u32[32]{0:T(128)} %constant.50) | copy-start | bytes 388
  11.8 10.0 %all-to-all-start.1 = ((bf16[4,8,1024]{2,1,0:T(8,128)(2,1)}), bf16[4,8,1024]{2,1,0:T(8,128)(2,1)S(1)}, u32[]{:S(2)}, u32[]{:S(2)}) async-start(bf16[4,8,1024]{2,1,0:T(8,128)(2,1)} %bitcast.3), calls=%async_computation.1 | async-start | bytes 131072 | tf_op jit(solution)/shard_map/all_to_all | solution.py:49
  22.4 8.1 %all-to-all-start.2 = ((bf16[4,8,1024]{2,1,0:T(8,128)(2,1)}), bf16[4,8,1024]{2,1,0:T(8,128)(2,1)S(1)}, u32[]{:S(2)}, u32[]{:S(2)}) async-start(bf16[4,8,1024]{2,1,0:T(8,128)(2,1)} %bitcast.6), calls=%async_computation.2 | async-start | bytes 131072 | tf_op jit(solution)/shard_map/all_to_all | solution.py:48
  30.5 7.8 %all-to-all-start = ((bf16[4,1,8]{2,1,0:T(2,128)(2,1)}), bf16[4,1,8]{2,1,0:T(2,128)(2,1)S(1)}, u32[]{:S(2)}, u32[]{:S(2)}) async-start(bf16[4,1,8]{2,1,0:T(2,128)(2,1)} %copy.45), calls=%async_computation | async-start | bytes 4096 | tf_op jit(solution)/shard_map/all_to_all | solution.py:50
  33.7 40.0 %all-reduce.8.cloned.1.call-start = ((), (), s32[]{:S(2)}) async-start(), calls=%async_computation.6 | async-start | bytes 262144 | tf_op jit(solution)/shard_map/psum | solution.py:65
  73.8 3.4 %copy-start.3 = (f32[64,256]{1,0:T(8,128)S(1)}, f32[64,256]{1,0:T(8,128)}, u32[]{:S(2)}) copy-start(f32[64,256]{1,0:T(8,128)} %get-tuple-element.20) | copy-start | bytes 196612
  82.3 8.2 %all-to-all-start.4 = ((f32[4,1,8]{2,1,0:T(1,128)}), f32[4,1,8]{2,1,0:T(1,128)S(1)}, u32[]{:S(2)}, u32[]{:S(2)}) async-start(f32[4,1,8]{2,1,0:T(1,128)} %bitcast.13), calls=%async_computation.4 | async-start | bytes 4096 | tf_op jit(solution)/shard_map/all_to_all | solution.py:87
  85.9 22.4 %all-reduce.6.cloned.1.call-start = ((), (), s32[]{:S(2)}) async-start(), calls=%async_computation.5 | async-start | bytes 524288
  110.5 8.9 %all-to-all-start.3 = ((f32[4,1,8,1024]{3,2,1,0:T(8,128)}), f32[4,1,8,1024]{3,2,1,0:T(8,128)S(1)}, u32[]{:S(2)}, u32[]{:S(2)}) async-start(f32[4,1,8,1024]{3,2,1,0:T(8,128)} %constant_dynamic-slice_fusion.1), calls=%async_computation.3 | async-start | bytes 262144 | tf_op jit(solution)/shard_map/all_to_all | solution.py:86
Sparse Core Ops, SparseCore 0:
  37.5 36.2 all-reduce.7
  89.7 18.5 all-reduce.5
where the time goes:
time: 136 us; the launch traced here: 135 us
  waiting for transfers between devices  55.6 us (41%)
  starting transfers between devices  19.2 us (14%)
  other arithmetic  17.3 us (13%)
  local copies, waits for them, and re-layouts  14.3 us (11%)
  between operations  14.2 us (10%)
  blocking collectives  8.02 us (6%)
  matrix products  6.81 us (5%)
    psum x1, waiting for transfers between devices, body(): pre_act, back_grad = lax.psum((pre_part, back_part), 'edata')  33 us
    gather x1, other arithmetic, body(): slot_gate[safe_index].reshape(tok_rows, 2)  10.1 us
    unnamed x3, waiting for transfers between devices  7.5 us
    unnamed x18, local copies, waits for them, and re-layouts  5.79 us
    all_to_all x1, starting transfers between devices, body(): lax.all_to_all(spread_dy, 'node', split_axis=0, concat_axis=0, tiled=True)  5.16 us
    reduce_sum x1, other arithmetic, body(): jnp.sum(jnp.where(keep_pair[:, :, None], picked, jnp.zeros((), jnp.float3...  4.96 us
    all_to_all x1, waiting for transfers between devices, body(): lax.all_to_all(reduced_x, 'node', split_axis=0, concat_axis=0, tiled=True)  4.34 us
    all_to_all x1, starting transfers between devices, body(): lax.all_to_all(reduced_x, 'node', split_axis=0, concat_axis=0, tiled=True)  3.91 us
  transfers between devices with their start and end apart: 7, of which 7 were waited for; matrix products, arithmetic and copies ran while one was open for 12% of the time, Pallas kernels for 0%

commit v1 on v0

v1 whole, which is shorter than its diff:
```python
import functools

import jax
import jax.numpy as jnp
from jax import lax
from jax.experimental import pallas as pl
from jax.experimental.pallas import tpu as pltpu
from jax.sharding import PartitionSpec as P

EXPERTS = 64
WINDOW = 2
GATE_LANES = 128
VMEM_LIMIT = 40 * 1024 * 1024

BF16 = jnp.bfloat16
F32 = jnp.float32


def gelu_pair(pre_act):
    coefficient = 0.7978845608028654
    square = pre_act * pre_act
    tanh_val = jnp.tanh(coefficient * (pre_act + 0.044715 * pre_act * square))
    half = 0.5 * (1.0 + tanh_val)
    activation = pre_act * half
    slopes = half + 0.5 * pre_act * (1.0 - tanh_val * tanh_val) * coefficient * (
        1.0 + 3.0 * 0.044715 * square
    )
    return (activation, slopes)


def call(kernel, out_shape, flops, moved):
    return pl.pallas_call(
        kernel,
        out_shape=out_shape,
        compiler_params=pltpu.CompilerParams(vmem_limit_bytes=VMEM_LIMIT),
        cost_estimate=pl.CostEstimate(flops=flops, bytes_accessed=moved, transcendentals=0),
    )


def gather_kernel(copies, routes_ref, gates_ref, tokens_ref, grads_ref, send_ref, place_ref):
    tok_rows = tokens_ref.shape[0]
    slots = place_ref.shape[0]
    capacity = slots // WINDOW
    routes = routes_ref[...]
    gates = gates_ref[...].astype(F32)
    named = []
    weight = []
    for expert in range(WINDOW):
        hit = (routes == expert).astype(F32)
        named.append(hit[0:1] + hit[1:2])
        scaled = hit * gates
        weight.append(scaled[0:1] + scaled[1:2])
    row_of = lax.broadcasted_iota(jnp.int32, (8, tok_rows), 0)
    names = jnp.where(row_of == 0, named[0], jnp.where(row_of == 1, named[1], 0.0)).astype(BF16)
    earlier = lax.broadcasted_iota(jnp.int32, (tok_rows, tok_rows), 0) < lax.broadcasted_iota(
        jnp.int32, (tok_rows, tok_rows), 1
    )
    before = jnp.dot(names, earlier.astype(F32).astype(BF16), preferred_element_type=F32)
    slot_of = lax.broadcasted_iota(jnp.int32, (capacity, tok_rows), 0).astype(F32)
    parts = [
        jnp.where(before[e : e + 1] == slot_of, named[e], 0.0) for e in range(WINDOW)
    ]
    place = jnp.concatenate(parts, axis=0)
    gated = jnp.concatenate([parts[e] * weight[e] for e in range(WINDOW)], axis=0)
    place_ref[...] = place.astype(BF16)
    rows_x = jnp.dot(place.astype(BF16), tokens_ref[...], preferred_element_type=F32)
    rows_dy = jnp.dot(gated.astype(BF16), grads_ref[...], preferred_element_type=F32)
    for expert in range(WINDOW):
        own = slice(expert * capacity, (expert + 1) * capacity)
        chunk = jnp.concatenate([rows_x[own], rows_dy[own]], axis=0).astype(BF16)
        for copy in range(copies):
            send_ref[expert * copies + copy] = chunk


def part_kernel(rows_ref, w_in_ref, w_out_ref, part_ref):
    groups, pair, feats = rows_ref.shape
    capacity = pair // 2
    hidden = w_in_ref.shape[1]
    rows = rows_ref[...].reshape(groups * pair, feats)
    pre = jnp.dot(rows, w_in_ref[...], preferred_element_type=F32)
    back = lax.dot_general(
        rows, w_out_ref[...], (((1,), (1,)), ((), ())), preferred_element_type=F32
    )
    pre = pre.reshape(groups, pair, hidden)[:, :capacity].reshape(groups * capacity, hidden)
    back = back.reshape(groups, pair, hidden)[:, capacity:].reshape(groups * capacity, hidden)
    part_ref[:, :hidden] = pre.astype(BF16)
    part_ref[:, hidden:] = back.astype(BF16)


def hidden_kernel(groups, parts_ref, w_in_ref, slot_ref, dpre_ref, act_ref):
    feats, hidden = w_in_ref.shape
    total = parts_ref[0].astype(F32)
    for index in range(1, parts_ref.shape[0]):
        total = total + parts_ref[index].astype(F32)
    pre, back = total[:, :hidden], total[:, hidden:]
    activation, slopes = gelu_pair(pre)
    dpre = back * slopes
    slot_ref[:, :feats] = lax.dot_general(
        dpre.astype(BF16), w_in_ref[...], (((1,), (1,)), ((), ())), preferred_element_type=F32
    ).astype(BF16)
    gate = jnp.sum(activation * back, axis=1, keepdims=True)
    high = gate.astype(BF16).astype(F32)
    lane = lax.broadcasted_iota(jnp.int32, (gate.shape[0], GATE_LANES), 1)
    slot_ref[:, feats:] = jnp.where(lane == 0, high, jnp.where(lane == 1, gate - high, 0.0)).astype(
        BF16
    )
    rows = dpre.shape[0]
    capacity = rows // groups
    dpre = dpre.reshape(groups, capacity, hidden)
    activation = activation.reshape(groups, capacity, hidden)
    blank = jnp.zeros_like(dpre)
    dpre_ref[...] = (
        jnp.concatenate([dpre, blank], axis=1).reshape(2 * rows, hidden).astype(BF16)
    )
    act_ref[...] = (
        jnp.concatenate([blank, activation], axis=1).reshape(2 * rows, hidden).astype(BF16)
    )


def combine_kernel(copies, came_ref, place_ref, routes_ref, gates_ref, tokens_ref, gate_out_ref):
    feats = tokens_ref.shape[1]
    slots = place_ref.shape[0]
    capacity = slots // WINDOW
    place = place_ref[...].astype(F32)
    spread = []
    for expert in range(WINDOW):
        own = place[expert * capacity : (expert + 1) * capacity]
        spread.append(jnp.concatenate([own] * copies, axis=0).astype(BF16))
    contract = (((0,), (0,)), ((), ()))
    tokens_ref[...] = lax.dot_general(
        jnp.concatenate(spread, axis=0), came_ref[:, :feats], contract, preferred_element_type=F32
    ).astype(BF16)
    routes = routes_ref[...]
    gates = gates_ref[...].astype(F32)
    result = jnp.zeros(gates.shape, F32)
    half = copies * capacity
    for expert in range(WINDOW):
        sums = lax.dot_general(
            came_ref[expert * half : (expert + 1) * half, feats:],
            spread[expert],
            contract,
            preferred_element_type=F32,
        )
        result = result + jnp.where(routes == expert, sums[0:1] + sums[1:2], 0.0)
    gate_out_ref[...] = result / gates


def body(tokens, grad_out, routes, gates, w_in, w_out):
    groups = lax.axis_size("node") * lax.axis_size("local")
    copies = groups // WINDOW
    tok_rows, feats = tokens.shape
    hidden = w_in.shape[1]
    capacity = 2 * tok_rows // EXPERTS
    slots = WINDOW * capacity
    rows = groups * capacity
    routes_t, gates_t = routes.T, gates.T
    send, place = call(
        functools.partial(gather_kernel, copies),
        (
            jax.ShapeDtypeStruct((groups, 2 * capacity, feats), BF16),
            jax.ShapeDtypeStruct((slots, tok_rows), BF16),
        ),
        4 * slots * tok_rows * feats,
        4 * tok_rows * feats + 4 * rows * feats,
    )(routes_t, gates_t, tokens, grad_out)
    got = lax.all_to_all(send, ("node", "local"), split_axis=0, concat_axis=0, tiled=True)
    part = call(
        part_kernel,
        jax.ShapeDtypeStruct((rows, 2 * hidden), BF16),
        8 * rows * feats * hidden,
        4 * rows * feats + 4 * feats * hidden,
    )(got, w_in, w_out)
    parts = lax.all_gather(part, "edata", axis=0)
    slot, dpre, act = call(
        functools.partial(hidden_kernel, groups),
        (
            jax.ShapeDtypeStruct((rows, feats + GATE_LANES), BF16),
            jax.ShapeDtypeStruct((2 * rows, hidden), BF16),
            jax.ShapeDtypeStruct((2 * rows, hidden), BF16),
        ),
        2 * rows * feats * hidden,
        2 * feats * hidden + 2 * rows * feats,
    )(parts, w_in)
    came = lax.all_to_all(
        slot.reshape(groups, capacity, feats + GATE_LANES),
        ("node", "local"),
        split_axis=0,
        concat_axis=0,
        tiled=True,
    )
    got_rows = got.reshape(2 * rows, feats)
    contract = (((0,), (0,)), ((), ()))
    grad_w_in = lax.dot_general(got_rows, dpre, contract, preferred_element_type=F32)
    grad_w_out = lax.dot_general(act, got_rows, contract, preferred_element_type=F32)
    grad_tokens, grad_gates = call(
        functools.partial(combine_kernel, copies),
        (
            jax.ShapeDtypeStruct((tok_rows, feats), BF16),
            jax.ShapeDtypeStruct((2, tok_rows), F32),
        ),
        2 * rows * tok_rows * feats,
        2 * rows * feats + 2 * tok_rows * feats,
    )(came.reshape(rows, feats + GATE_LANES), place, routes_t, gates_t)
    return (grad_tokens, grad_gates.T, grad_w_in, grad_w_out)


def solution(mesh):
    in_specs = (
        P(("node", "local"), "edata"),
        P(("node", "local"), "edata"),
        P(("node", "local"), None),
        P(("node", "local"), None),
        P("edata", ("node", "local")),
        P(("node", "local"), "edata"),
    )
    out_specs = (
        P(("node", "local"), "edata"),
        P(("node", "local"), None),
        P("edata", ("node", "local")),
        P(("node", "local"), "edata"),
    )
    return jax.shard_map(body, mesh=mesh, in_specs=in_specs, out_specs=out_specs, check_vma=False)
```

time: 136 us -> 41.8 us (0.31)
  waiting for transfers between devices: 55.6 us -> 3.05 us
  blocking collectives: 8.02 us -> 26.2 us
  other arithmetic: 17.3 us -> 0 us
  starting transfers between devices: 19.2 us -> 3.38 us
  between operations: 14.2 us -> 0.67 us
  local copies, waits for them, and re-layouts: 14.3 us -> 2.77 us
  matrix products: 6.81 us -> 2.58 us
  Pallas kernels: 0 us -> 2.79 us
    psum x1 -> x0, waiting for transfers between devices: 33 us -> none  [body(): pre_act, back_grad = lax.psum((pre_part, back_part), 'edata')]
    all_to_all x5 -> x1, starting transfers between devices: 19.2 us -> 3.38 us  [body(): lax.all_to_all(slot.reshape(groups, capacity, feats + GATE_LANES), ('node...]
    all_to_all x5 -> x1, waiting for transfers between devices: 15.1 us -> 3.05 us  [body(): lax.all_to_all(slot.reshape(groups, capacity, feats + GATE_LANES), ('node...]
    all_to_all x0 -> x1, blocking collectives: none -> 12 us  [body(): lax.all_to_all(send, ('node', 'local'), split_axis=0, concat_axis=0, tile...]
    gather x2 -> x0, other arithmetic: 10.1 us -> none  [the longest x1 10.1 us: body(): slot_gate[safe_index].reshape(tok_rows, 2)]
    all_gather x3 -> x1, blocking collectives: 5.57 us -> 14.1 us  [body(): parts = lax.all_gather(part, 'edata', axis=0)]
    unnamed x3 -> x0, waiting for transfers between devices: 7.5 us -> none
    reduce_sum x6 -> x0, other arithmetic: 6.23 us -> none  [the longest x1 4.96 us: body(): jnp.sum(jnp.where(keep_pair[:, :, None], picked, jnp.zeros((), jnp.float3...]
  transfers between devices with their start and end apart: 7 -> 1, of which waited for: 7 -> 1; matrix products, arithmetic and copies ran while one was open for 12% -> 6% of each run, Pallas kernels for 0% -> 0%
where the time goes in v1:
time: 41.8 us; the launch traced here: 41.4 us
  blocking collectives  26.2 us (63%)
  starting transfers between devices  3.38 us (8%)
  waiting for transfers between devices  3.05 us (7%)
  Pallas kernels  2.79 us (7%)
  local copies, waits for them, and re-layouts  2.77 us (7%)
  matrix products  2.58 us (6%)
  between operations  0.67 us (2%)
    all_gather x1, blocking collectives, body(): parts = lax.all_gather(part, 'edata', axis=0)  14.1 us
    all_to_all x1, blocking collectives, body(): lax.all_to_all(send, ('node', 'local'), split_axis=0, concat_axis=0, tile...  12 us
    all_to_all x1, starting transfers between devices, body(): lax.all_to_all(slot.reshape(groups, capacity, feats + GATE_LANES), ('node...  3.38 us
    all_to_all x1, waiting for transfers between devices, body(): lax.all_to_all(slot.reshape(groups, capacity, feats + GATE_LANES), ('node...  3.05 us
    unnamed x12, local copies, waits for them, and re-layouts  2.77 us
    dot_general x1, matrix products, body(): lax.dot_general(got_rows, dpre, contract, preferred_element_type=F32)  1.29 us
    dot_general x1, matrix products, body(): lax.dot_general(act, got_rows, contract, preferred_element_type=F32)  1.29 us
    pallas_call x1, Pallas kernels, body(): call(functools.partial(combine_kernel, copies), (jax.ShapeDtypeStruct((to...  1.11 us
  transfers between devices with their start and end apart: 1, of which 1 were waited for; matrix products, arithmetic and copies ran while one was open for 6% of the time, Pallas kernels for 0%

profile of v1, /device:TPU:0, one launch (start us, length us, event | category | flops | bytes accessed | tf_op | source)
XLA Modules:
  0.0 41.4 jit_solution(3446742243421762311)
XLA Ops:
  0.6 0.0 copy-start.4
  0.6 0.0 copy-start.5
  0.7 0.7 %copy-done.4 = s32[256,2]{0,1:T(2,128)S(1)} copy-done((s32[256,2]{0,1:T(2,128)S(1)}, s32[256,2]{0,1:T(2,128)}, u32[]{:S(2)}) %copy-start.4) | copy-done | bytes 2072
  1.3 0.0 copy-done.5
  1.3 0.0 copy-start.1
  1.3 1.0 %copy-done.1 = bf16[256,1024]{1,0:T(8,128)(2,1)S(1)} copy-done((bf16[256,1024]{1,0:T(8,128)(2,1)S(1)}, bf16[256,1024]{1,0:T(8,128)(2,1)}, u32[]{:S(2)}) %copy-start.1) | copy-done | bytes 524312
  2.4 0.0 copy-start.2
  2.4 1.0 %copy-done.2 = bf16[256,1024]{1,0:T(8,128)(2,1)S(1)} copy-done((bf16[256,1024]{1,0:T(8,128)(2,1)S(1)}, bf16[256,1024]{1,0:T(8,128)(2,1)}, u32[]{:S(2)}) %copy-start.2) | copy-done | bytes 524312
  3.4 0.0 copy-start.3
  3.4 0.4 shard_map.93
  3.8 0.0 copy-start
  3.8 12.0 %all_to_all.10.rows_ref = bf16[8,16,1024]{2,1,0:T(8,128)(2,1)S(1)} all-to-all(bf16[8,16,1024]{2,1,0:T(8,128)(2,1)S(1)} %get-tuple-element.11), channel_id=1, replica_groups=mesh['node'=4,'local'=2,'edata'=4] {'node','local'}, dimensions={0} | all-to-all | bytes 524288 | tf_op jit(solution)/shard_map/all_to_all | solution.py:166
  15.8 0.0 copy-done.3
  15.8 0.0 copy-done
  15.8 0.4 shard_map.94
  16.2 14.1 %all-gather = bf16[256,512]{1,0:T(8,128)(2,1)S(1)} all-gather(bf16[64,512]{1,0:T(8,128)(2,1)S(1)} %shard_map.94), channel_id=2, replica_groups=mesh['node'=4,'local'=2,'edata'=4] {'edata'}, dimensions={0}, use_global_device_ids=true | all-gather | bytes 327680 | tf_op jit(solution)/shard_map/all_gather | solution.py:173
  30.3 0.9 %shard_map.95 = (bf16[64,1152]{1,0:T(8,128)(2,1)}, bf16[128,256]{1,0:T(8,128)(2,1)S(1)}, bf16[128,256]{1,0:T(8,128)(2,1)S(1)}) custom-call(bf16[4,64,512]{2,1,0:T(8,128)(2,1)S(1)} %bitcast.13, bf16[1024,256]{1,0:T(8,128)(2,1)S(1)} %copy-done), custom_call_target="tpu_custom_call" | custom-call | flops 33554432 | bytes 655360 | tf_op jit(solution)/shard_map/pallas_call | solution.py:174
  31.3 3.4 %all-to-all-start.1 = ((bf16[8,8,1152]{2,1,0:T(8,128)(2,1)}), bf16[8,8,1152]{2,1,0:T(8,128)(2,1)S(1)}, u32[]{:S(2)}, u32[]{:S(2)}) async-start(bf16[8,8,1152]{2,1,0:T(8,128)(2,1)} %bitcast.3), calls=%async_computation.1 | async-start | bytes 294912 | tf_op jit(solution)/shard_map/all_to_all | solution.py:184
  34.7 1.3 %fusion = f32[1024,256]{1,0:T(8,128)} fusion(bf16[128,1024]{1,0:T(8,128)(2,1)S(1)} %bitcast.11, bf16[128,256]{1,0:T(8,128)(2,1)S(1)} %get-tuple-element.16), kind=kOutput, calls=%fused_computation | convolution fusion | flops 67108864 | bytes 1376256 | tf_op jit(solution)/shard_map/dot_general | solution.py:193
  36.0 1.3 %fusion.1 = f32[256,1024]{1,0:T(8,128)} fusion(bf16[128,256]{1,0:T(8,128)(2,1)S(1)} %get-tuple-element.17, bf16[128,1024]{1,0:T(8,128)(2,1)S(1)} %bitcast.12), kind=kOutput, calls=%fused_computation.1 | convolution fusion | flops 67108864 | bytes 1376256 | tf_op jit(solution)/shard_map/dot_general | solution.py:194
  37.3 3.1 %all-to-all-done.1 = bf16[8,8,1152]{2,1,0:T(8,128)(2,1)S(1)} async-done(((bf16[8,8,1152]{2,1,0:T(8,128)(2,1)}), bf16[8,8,1152]{2,1,0:T(8,128)(2,1)S(1)}, u32[]{:S(2)}, u32[]{:S(2)}) %all-to-all-start.1) | async-done | bytes 147488 | tf_op jit(solution)/shard_map/all_to_all | solution.py:184
  40.3 1.1 %shard_map.96 = (bf16[256,1024]{1,0:T(8,128)(2,1)}, f32[2,256]{1,0:T(2,128)}) custom-call(bf16[64,1152]{1,0:T(8,128)(2,1)S(1)} %bitcast.14, bf16[16,256]{1,0:T(8,128)(2,1)S(1)} %get-tuple-element.13.place_ref, s32[2,256]{1,0:T(2,128)S(1)} %bitcast.16, bf16[2,256]{1,0:T(2,128)(2,1)S(1)} %bitcast.18), custom_call_target="tpu_custom_call" | custom-call | flops 33554432 | bytes 655360 | tf_op jit(solution)/shard_map/pallas_call | solution.py:195
Async XLA Ops:
  0.6 0.7 %copy-start.4 = (s32[256,2]{0,1:T(2,128)S(1)}, s32[256,2]{0,1:T(2,128)}, u32[]{:S(2)}) copy-start(s32[256,2]{0,1:T(2,128)} %param.8) | copy-start | bytes 6148
  0.6 0.7 %copy-start.5 = (bf16[256,2]{0,1:T(2,128)(2,1)S(1)}, bf16[256,2]{0,1:T(2,128)(2,1)}, u32[]{:S(2)}) copy-start(bf16[256,2]{0,1:T(2,128)(2,1)} %param.9) | copy-start | bytes 3076
  1.3 1.0 %copy-start.1 = (bf16[256,1024]{1,0:T(8,128)(2,1)S(1)}, bf16[256,1024]{1,0:T(8,128)(2,1)}, u32[]{:S(2)}) copy-start(bf16[256,1024]{1,0:T(8,128)(2,1)} %tokens_ref.1) | copy-start | bytes 1572868
  2.4 1.0 %copy-start.2 = (bf16[256,1024]{1,0:T(8,128)(2,1)S(1)}, bf16[256,1024]{1,0:T(8,128)(2,1)}, u32[]{:S(2)}) copy-start(bf16[256,1024]{1,0:T(8,128)(2,1)} %grads_ref.1) | copy-start | bytes 1572868
  3.4 12.4 %copy-start.3 = (bf16[256,1024]{1,0:T(8,128)(2,1)S(1)}, bf16[256,1024]{1,0:T(8,128)(2,1)}, u32[]{:S(2)}) copy-start(bf16[256,1024]{1,0:T(8,128)(2,1)} %w_out_ref.1) | copy-start | bytes 1572868
  3.8 12.0 %copy-start = (bf16[1024,256]{1,0:T(8,128)(2,1)S(1)}, bf16[1024,256]{1,0:T(8,128)(2,1)}, u32[]{:S(2)}) copy-start(bf16[1024,256]{1,0:T(8,128)(2,1)} %w_in_ref.3) | copy-start | bytes 1572868
  31.3 9.0 %all-to-all-start.1 = ((bf16[8,8,1152]{2,1,0:T(8,128)(2,1)}), bf16[8,8,1152]{2,1,0:T(8,128)(2,1)S(1)}, u32[]{:S(2)}, u32[]{:S(2)}) async-start(bf16[8,8,1152]{2,1,0:T(8,128)(2,1)} %bitcast.3), calls=%async_computation.1 | async-start | bytes 294912 | tf_op jit(solution)/shard_map/all_to_all | solution.py:184
